TPU v7x, 512 devices: a whole 4x8x8 slice. The times are simulated.
512 devices in a mesh: island: 16 (over z_hi, y), fsdp: 32 (over z_lo, x, core).
Axes of the slice: x: 4, y: 8, z: 8 (z_hi: 2, z_lo: 4; z = z_hi * 4 + z_lo), core: 2. Of those that a mesh axis runs over, the one named last changes fastest.
Arguments:
- activations: bfloat16 [98304, 8192], P(('island', 'fsdp')), may hold values from -6 to 6
- local_weights: bfloat16 [16, 8192, 512], P('island', 'fsdp'), may hold values from -0.0625 to 0.0625
- grad_codes: int32 [16, 8192, 512], P('island', 'fsdp'), may hold values from -8 to 7
- block_scales: float32 [16, 8192, 4], P('island', 'fsdp'), may hold values from 0.03 to 0.5
- global_weights: bfloat16 [8192, 512], P('fsdp'), may hold values from -3 to 3
- momentum: bfloat16 [16, 8192, 512], P('island', 'fsdp'), may hold values from -3 to 3
- block_owner: int32 [8192, 4], P('fsdp'), may hold values from 0 to 15
Outputs:
- projected_keys: bfloat16 [98304, 512], P(('island', 'fsdp'))
- new_global: bfloat16 [8192, 512], P('fsdp')
- new_momentum: bfloat16 [8192, 512], P('fsdp')
Inputs may be any that keep to these rules, and one draw needn't show every extreme that they name: `grad_codes`: codes of a signed 4-bit quantizer.
All inputs are finite; a program needn't handle non-finite values.
Results may differ from a plain program's by a relative error of at most 0.001.
Values may be sent and summed in bfloat16 or wider, within the bound.
A program may use at most 64 MiB of HBM per device.

v0:
```python
import jax
import jax.numpy as jnp
from jax import lax
from jax.sharding import PartitionSpec as P

outer_momentum = 0.9
outer_rate = 0.7


def outer_step(global_f32, mean_delta, held_state):
    fresh = outer_momentum * held_state + mean_delta
    updated = (global_f32 - outer_rate * (mean_delta + outer_momentum * fresh)).astype(jnp.bfloat16)
    return (updated, fresh.astype(jnp.bfloat16))


def body(
    activations, local_weights, grad_codes, block_scales, global_weights, momentum, block_owner
):
    key_width = local_weights.shape[2]
    projected = jnp.dot(
        activations,
        lax.all_gather(local_weights[0], "fsdp", axis=0, tiled=True),
        preferred_element_type=jnp.float32,
    ).astype(jnp.bfloat16)
    islands = lax.axis_size("island")
    my_island = lax.axis_index("island")
    row_count = grad_codes.shape[1]
    block_count = block_scales.shape[2]
    block_size = key_width // block_count
    pseudo = (
        grad_codes[0].reshape(row_count, block_count, block_size).astype(jnp.float32)
        * block_scales[0][..., None]
    )
    stored_half = momentum[0].reshape(row_count, block_count, block_size)
    owned_mask = (block_owner == my_island)[..., None]
    global_f32 = global_weights.reshape(row_count, block_count, block_size).astype(jnp.float32)
    summed = lax.psum(pseudo, "island")
    local_global, local_state = outer_step(
        global_f32, summed / islands, stored_half.astype(jnp.float32)
    )
    global_terms = jnp.where(owned_mask, local_global, jnp.zeros_like(local_global))
    state_terms = jnp.where(owned_mask, local_state, jnp.zeros_like(local_state))
    global_sum, state_sum = (
        lax.psum(global_terms, "island").astype(jnp.float32),
        lax.psum(state_terms, "island").astype(jnp.float32),
    )
    new_global = global_sum.astype(jnp.bfloat16)
    new_momentum = state_sum.astype(jnp.bfloat16)
    return (
        projected,
        new_global.reshape(row_count, key_width),
        new_momentum.reshape(row_count, key_width),
    )


def solution(mesh):
    return jax.shard_map(
        body,
        mesh=mesh,
        in_specs=(
            P(("island", "fsdp"), None),
            P("island", "fsdp", None),
            P("island", "fsdp", None),
            P("island", "fsdp", None),
            P("fsdp", None),
            P("island", "fsdp", None),
            P("fsdp", None),
        ),
        out_specs=(P(("island", "fsdp"), None), P("fsdp", None), P("fsdp", None)),
        check_vma=False,
    )
```

profile of v0, /device:TPU:2, one launch (start us, length us, event | category | flops | bytes accessed | tf_op | source)
XLA Modules:
  0.0 424.0 jit_solution(13152205389293496711)
XLA Ops:
  8.0 0.0 copy-start
  8.0 0.0 all-reduce.4.cloned.1.call-start
  8.1 2.0 convert_element_type.32
  10.1 2.0 convert_element_type.33
  12.1 0.8 copy.11
  12.9 2.2 broadcast_multiply_fusion
  15.1 0.0 all-reduce.4.cloned.1.call-update
  15.1 0.0 all-gather.3.cloned.1.call-start
  15.2 0.5 all-gather.3.cloned.1.call-update
  15.7 0.0 all-reduce.6.cloned.1.call-start
  15.7 1.8 convert_multiply_fusion
  17.6 2.1 mul.29
  19.6 0.7 broadcast_compare_fusion
  20.3 0.2 copy.10
  20.5 1.9 reshape.23
  22.4 194.0 %all-reduce.4.cloned.1.call-done = f32[256,4,128]{2,1,0:T(4,128)} async-done(((f32[256,4,128]{2,1,0:T(4,128)}), f32[256,4,128]{2,1,0:T(4,128)}) %all-reduce.4.cloned.1.call-update) | async-done | bytes 524304 | tf_op jit(solution)/shard_map/psum | solution.py:37
  216.4 1.7 fusion.6
  218.1 0.9 copy_bitcast_fusion
  218.9 0.0 all-reduce.6.cloned.1.call-update
  218.9 0.0 all-gather.3.cloned.1.call-done
  219.0 5.8 %fusion.2 = bf16[192,512]{1,0:T(8,128)(2,1)} fusion(bf16[192,8192]{1,0:T(8,128)(2,1)S(1)} %copy-done, bf16[1,8192,512]{2,1,0:T(8,128)(2,1)} %all-gather.3.cloned.1.call-done), kind=kOutput, calls=%fused_computation.2 | convolution fusion | flops 1610711040 | bytes 11730944 | tf_op jit(solution)/shard_map/dot_general | solution.py:20
  224.8 188.4 %all-reduce.6.cloned.1.call-done = (bf16[256,512]{1,0:T(8,128)(2,1)}, bf16[256,512]{1,0:T(8,128)(2,1)}) async-done(((bf16[256,512]{1,0:T(8,128)(2,1)}, bf16[256,512]{1,0:T(8,128)(2,1)}), (bf16[256,512]{1,0:T(8,128)(2,1)}, bf16[256,512]{1,0:T(8,128)(2,1)})) %all-reduce.6.cloned.1.call-update) | async-done | bytes 524304 | tf_op jit(solution)/shard_map/psum | solution.py:44
  413.3 1.7 copy.19
  414.9 1.7 copy.20
  (1 shorter events, 0.0 us)
Async XLA Ops:
  8.0 211.0 %copy-start = (bf16[192,8192]{1,0:T(8,128)(2,1)S(1)}, bf16[192,8192]{1,0:T(8,128)(2,1)}, u32[]{:S(2)}) copy-start(bf16[192,8192]{1,0:T(8,128)(2,1)} %param.7) | copy-start | bytes 9437188
  8.0 208.4 %all-reduce.4.cloned.1.call-start = ((), (), s32[]{:S(2)}) async-start(), calls=%async_computation | async-start | bytes 1048576 | tf_op jit(solution)/shard_map/psum | solution.py:37
  15.1 203.8 %all-gather.3.cloned.1.call-start = ((), (), s32[]{:S(2)}) async-start(), calls=%async_computation.1 | async-start | bytes 8650752 | tf_op jit(solution)/shard_map/all_gather | solution.py:22
  15.7 397.6 %all-reduce.6.cloned.1.call-start = ((), (), s32[]{:S(2)}) async-start(), calls=%async_computation.2 | async-start | bytes 1048576 | tf_op jit(solution)/shard_map/psum | solution.py:44
Sparse Core Ops, SparseCore 0:
  15.2 201.0 all-reduce.3
  220.1 193.0 all-reduce.5
Sparse Core Ops, SparseCore 1:
  17.7 77.9 all-gather.2
where the time goes:
time: 425 us; the launch traced here: 424 us
  waiting for transfers between devices  383 us (90%)
  between operations  15.5 us (4%)
  local copies, waits for them, and re-layouts  11.2 us (3%)
  other arithmetic  8.4 us (2%)
  matrix products  5.85 us (1%)
    psum x1, waiting for transfers between devices, body(): summed = lax.psum(pseudo, 'island')  194 us
    psum x1, waiting for transfers between devices, body(): lax.psum(global_terms, 'island').astype(jnp.float32)  188 us
  transfers between devices with their start and end apart: 3, of which 2 were waited for; matrix products, arithmetic and copies ran while one was open for 4% of the time, Pallas kernels for 0%

commit v1 on v0

v1 whole, which is shorter than its diff:
```python
import functools

import jax
import jax.numpy as jnp
from jax import lax
from jax.experimental import pallas as pl
from jax.experimental.pallas import tpu as pltpu
from jax.sharding import PartitionSpec as P

MESH = pl.DeviceIdType.MESH

outer_momentum = 0.9
outer_rate = 0.7

NX, NZ, NY = 4, 4, 8
Q = 32


def gather_kernel(
    act, wown, codes, scales, owner, gw, mom,
    proj, og, om,
    X, W, acc, pacc,
    cbuf, stg, rbuf, scbuf, rsc, owbuf, gbuf, tmp, tmpt, zs, zm, zrs, zrm, res,
    lsem, zsem_s, zsem_r, xsem_s, xsem_r, qxs, qxr, qzs, qzr,
    acts, actr, pts, ptr_, rss, rsr, scs, scr, zhs, zhr, ags, agr, osem,
):
    i, f = lax.axis_index("island"), lax.axis_index("fsdp")
    zh, y = i // NY, i % NY
    z, x, c = f // (2 * NX), (f // 2) % NX, f % 2
    rows = wown.shape[0]
    p = rows - Q
    hp = p // 2
    tok = act.shape[0]
    depth = rows

    def fs(zz, xx, cc):
        return {"fsdp": zz * 2 * NX + xx * 2 + cc}

    def isl(hh, yy):
        return {"island": hh * NY + yy}

    xl, xr, xo = (x + NX - 1) % NX, (x + 1) % NX, (x + 2) % NX
    right, left = fs(z, xr, c), fs(z, xl, c)
    partner = fs(z, x, 1 - c)
    far = isl(1 - zh, y)

    def rcopy(src, dst, ss, rs, dev):
        return pltpu.make_async_remote_copy(
            src_ref=src, dst_ref=dst, send_sem=ss, recv_sem=rs, device_id=dev, device_id_type=MESH
        )

    kown = z * NX + x
    ld_codes = pltpu.make_async_copy(codes, cbuf, lsem.at[0])
    ld_codes.start()
    ld_w = pltpu.make_async_copy(wown, W.at[kown], lsem.at[1])
    ld_w.start()
    ld_mom = pltpu.make_async_copy(mom, stg.at[:, :, pl.ds(16, 16), :], lsem.at[2])
    ld_mom.start()
    ld_sc = pltpu.make_async_copy(scales, scbuf, lsem.at[3])
    ld_sc.start()
    ld_ow = pltpu.make_async_copy(owner, owbuf, lsem.at[4])
    ld_ow.start()
    ld_gw = pltpu.make_async_copy(gw.at[y], gbuf, lsem.at[5])
    ld_gw.start()

    @pl.loop(0, NX * NZ)
    def _(k):
        col = pl.multiple_of((2 * k + c) * depth, depth)
        pltpu.make_async_copy(
            act.at[:, pl.ds(col, depth)], X.at[k, pl.ds(0, tok), :], lsem.at[6]
        ).start()

    bar = pltpu.get_barrier_semaphore()
    zg = zh * NZ + z
    zup, zdn = (zg + 1) % (2 * NZ), (zg + 2 * NZ - 1) % (2 * NZ)
    peers = [right, left, partner, far]
    peers += [isl(zh, (y + d) % NY) for d in range(1, NY)]
    peers += [
        {"island": (n // NZ) * NY + y, "fsdp": (n % NZ) * 2 * NX + x * 2 + c} for n in (zup, zdn)
    ]
    for dev in peers:
        pl.semaphore_signal(bar, inc=1, device_id=dev, device_id_type=MESH)

    ld_codes.wait()

    @pl.loop(0, NY)
    def _(t):
        stg[t, :, pl.ds(0, 16), :] = cbuf[t].astype(jnp.float32).astype(jnp.bfloat16)

    ld_w.wait()
    ld_mom.wait()
    ld_sc.wait()
    pl.semaphore_wait(bar, len(peers))

    def half(k, h):
        return W.at[k, pl.ds(h * hp, hp), :]

    def qpart(k):
        return W.at[k, pl.ds(p, Q), :]

    def qhalf(k, h):
        return W.at[k, pl.ds(p + h * (Q // 2), Q // 2), :]

    def qrow(r):
        return W.at[pl.ds(r * NX, NX), pl.ds(p, Q), :]

    m = z // 2
    e = z * (1 - m) + (NZ - 1 - z) * m

    def order(j):
        g = j if j >= 2 else j * (1 - e) + (1 - j) * e
        return g * (1 - m) + (NZ - 1 - g) * m

    def xcopy(j, n):
        r = order(j) * NX
        k, h, dev = [
            (r + x, 0, right), (r + x, 1, right), (r + x, 1, left), (r + x, 0, left),
            (r + xl, 0, right), (r + xr, 1, left),
        ][n]
        return rcopy(half(k, h), half(k, h), xsem_s.at[j, n], xsem_r.at[j, n], dev)

    def xlanded(j, n):
        r = order(j) * NX
        k, h = [(r + xl, 0), (r + xl, 1), (r + xr, 1), (r + xr, 0), (r + xo, 0), (r + xo, 1)][n]
        return rcopy(half(k, h), half(k, h), xsem_s.at[j, n], xsem_r.at[j, n], right)

    def qxcopy(n):
        k = [kown, kown, z * NX + xl, z * NX + xr][n]
        dev = [right, left, right, left][n]
        ref = qpart(k) if n < 2 else qhalf(k, n - 2)
        return rcopy(ref, ref, qxs.at[n], qxr.at[n], dev)

    def qxlanded(n):
        k = z * NX + [xl, xr, xo, xo][n]
        ref = qpart(k) if n < 2 else qhalf(k, n - 2)
        return rcopy(ref, ref, qxs.at[n], qxr.at[n], right)

    up, down = fs(z + 1, x, c), fs(z - 1, x, c)

    def zcopy(s, h, d):
        k = (z - s if d == 0 else z + s) * NX + x
        return rcopy(half(k, h), half(k, h), zsem_s.at[s, h, d], zsem_r.at[s, h, d], up if d == 0 else down)

    def zlanded(s, h, d):
        k = (z - s if d == 0 else z + s) * NX + x
        return rcopy(half(k, h), half(k, h), zsem_s.at[s - 1, h, d], zsem_r.at[s - 1, h, d], up if d == 0 else down)

    def qzcopy(s, d):
        ref = qrow(z - s if d == 0 else z + s)
        return rcopy(ref, ref, qzs.at[s, d], qzr.at[s, d], up if d == 0 else down)

    def qzlanded(s, d):
        ref = qrow(z - s if d == 0 else z + s)
        return rcopy(ref, ref, qzs.at[s - 1, d], qzr.at[s - 1, d], up if d == 0 else down)

    def has(s, d):
        return z - s >= 0 if d == 0 else z + s <= NZ - 1

    def goes(d):
        return z < NZ - 1 if d == 0 else z > 0

    def zpass(s):
        for h in range(2):
            for d in range(2):
                @pl.when(has(s, d))
                def _():
                    zlanded(s, h, d).wait_recv()

                    @pl.when(goes(d))
                    def _():
                        zcopy(s, h, d).start()

    def qzpass(s):
        for d in range(2):
            @pl.when(has(s, d))
            def _():
                qzlanded(s, d).wait_recv()

                @pl.when(goes(d))
                def _():
                    qzcopy(s, d).start()

    def xsend(j):
        for n in (0, 2, 1, 3):
            xcopy(j, n).start()

    def xpass(j):
        for n in (0, 2):
            xlanded(j, n).wait_recv()
            xcopy(j, 4 + n // 2).start()

    def xdone(j):
        for n in (1, 3, 4, 5):
            xlanded(j, n).wait_recv()

    def multiply(k, first=False):
        part = jnp.dot(X[k], W[k], preferred_element_type=jnp.float32)
        if first:
            acc[...] = part
        else:
            acc[...] += part

    def multiply_row(j):
        r = order(j) * NX

        @pl.loop(0, NX)
        def _(n):
            multiply(r + n)

    def rs_copy(hf, d):
        t = (y + d) % NY
        return rcopy(stg.at[t, hf], rbuf.at[hf, d - 1], rss.at[hf], rsr.at[hf], isl(zh, t))

    def sc_copy(d):
        t = (y + d) % NY
        lanes = pl.ds(pl.multiple_of((t // 4) * 128, 128), 128)
        return rcopy(scbuf.at[:, lanes], rsc.at[d - 1], scs, scr, isl(zh, t))

    def zh_copies(hf):
        return (
            rcopy(zs.at[hf], zrs.at[hf], zhs.at[hf, 0], zhr.at[hf, 0], far),
            rcopy(zm.at[hf], zrm.at[hf], zhs.at[hf, 1], zhr.at[hf, 1], far),
        )

    def ag_copy(hf, d):
        return rcopy(res.at[hf, y], res.at[hf, y], ags.at[hf], agr.at[hf], isl(zh, (y + d) % NY))

    far_first = (4, 3, 5, 2, 6, 1, 7)

    def small_columns():
        rcopy(rsc, rsc, scs, scr, far).wait_recv()
        ld_ow.wait()
        lanes = pl.ds(pl.multiple_of((y // 4) * 128, 128), 128)
        tmp[...] = jnp.zeros_like(tmp)
        tmp[pl.ds(0, 4), :] = scbuf[:, lanes]
        for d in range(1, NY):
            tmp[pl.ds(4 * d, 4), :] = rsc[d - 1]
        tmp[pl.ds(32, 4), :] = owbuf[:, lanes].astype(jnp.float32)
        tmpt[...] = tmp[...].T

    def partial(hf):
        rcopy(rbuf.at[hf], rbuf.at[hf], rss.at[hf], rsr.at[hf], far).wait_recv()
        cols = tmpt[pl.ds(pl.multiple_of(32 * (y % 4) + 16 * hf, 16), 16), :]
        for b in range(4):
            lanes = pl.ds(128 * b, 128)
            total = jnp.zeros((16, 128), jnp.float32)
            held = jnp.zeros((16, 128), jnp.float32)
            own = jnp.broadcast_to(cols[:, 32 + b : 33 + b], (16, 128))
            for d in range(NY):
                if d == 0:
                    code, state = stg[y, hf, pl.ds(0, 16), lanes], stg[y, hf, pl.ds(16, 16), lanes]
                else:
                    code, state = (
                        rbuf[hf, d - 1, pl.ds(0, 16), lanes],
                        rbuf[hf, d - 1, pl.ds(16, 16), lanes],
                    )
                total += code.astype(jnp.float32) * cols[:, 4 * d + b : 4 * d + b + 1]
                who = (zh * NY + (y + NY - d) % NY).astype(jnp.float32)
                held += jnp.where(own == who, state.astype(jnp.float32), 0.0)
            zs[hf, :, lanes] = total
            zm[hf, :, lanes] = held.astype(jnp.bfloat16)
        for cp in zh_copies(hf):
            cp.start()

    def finish(hf):
        for cp in zh_copies(hf):
            cp.wait_recv()
        mean = (zs[hf] + zrs[hf]) * (1.0 / (2 * NY))
        held = zm[hf].astype(jnp.float32) + zrm[hf].astype(jnp.float32)
        fresh = outer_momentum * held + mean
        updated = gbuf[hf].astype(jnp.float32) - outer_rate * (mean + outer_momentum * fresh)
        res[hf, y, 0] = updated.astype(jnp.bfloat16)
        res[hf, y, 1] = fresh.astype(jnp.bfloat16)
        for d in far_first:
            ag_copy(hf, d).start()

    qxcopy(0).start()
    qxcopy(1).start()
    xsend(0)
    for h in range(2):
        for d in range(2):
            @pl.when(goes(d))
            def _():
                zcopy(0, h, d).start()
    for hf in range(2):
        for d in far_first:
            rs_copy(hf, d).start()
        if hf == 0:
            for d in far_first:
                sc_copy(d).start()

    @pl.loop(0, NX * NZ)
    def _(k):
        col = pl.multiple_of((2 * k + 1 - c) * depth, depth)
        rcopy(act.at[:, pl.ds(col, depth)], X.at[k, pl.ds(tok, tok), :], acts, actr, partner).start()

    for n in range(2):
        qxlanded(n).wait_recv()
        qxcopy(2 + n).start()
    zpass(1)
    xsend(1)
    xpass(0)
    for n in (2, 3):
        qxlanded(n).wait_recv()
    for d in range(2):
        @pl.when(goes(d))
        def _():
            qzcopy(0, d).start()
    small_columns()
    partial(0)
    zpass(2)
    xsend(2)
    xpass(1)
    xdone(0)
    rcopy(X.at[:, pl.ds(tok, tok), :], X.at[:, pl.ds(tok, tok), :], acts, actr, partner).wait_recv()
    pltpu.make_async_copy(X.at[:, pl.ds(0, tok), :], X.at[:, pl.ds(0, tok), :], lsem.at[6]).wait()
    acc[...] = jnp.zeros_like(acc)
    partial(1)
    zpass(3)
    xsend(3)
    multiply_row(0)
    qzpass(1)
    xpass(2)
    ld_gw.wait()
    finish(0)
    qzpass(2)
    xdone(1)
    qzpass(3)
    multiply_row(1)
    xpass(3)
    finish(1)
    xdone(2)
    multiply_row(2)
    xdone(3)
    multiply_row(3)

    pcopy = rcopy(acc.at[pl.ds(tok, tok), :], pacc, pts, ptr_, partner)
    pcopy.start()
    for hf in range(2):
        rcopy(res.at[hf, pl.ds(0, 7)], res.at[hf, pl.ds(0, 7)], ags.at[hf], agr.at[hf], far).wait_recv()
    outs = []
    for hf in range(2):
        for n, out in enumerate((og, om)):
            cp = pltpu.make_async_copy(res.at[hf, :, n], out.at[:, hf], osem.at[hf, n])
            cp.start()
            outs.append(cp)
    pcopy.wait_recv()
    proj[...] = (acc[pl.ds(0, tok), :] + pacc[...]).astype(jnp.bfloat16)

    for j in range(NZ):
        for n in range(6):
            xcopy(j, n).wait_send()
    for n in range(4):
        qxcopy(n).wait_send()
    for s in range(NZ):
        for d in range(2):
            if s < NZ - 1:
                @pl.when(has(s, d) & goes(d))
                def _():
                    for h in range(2):
                        zcopy(s, h, d).wait_send()
                    qzcopy(s, d).wait_send()
    rcopy(X.at[:, pl.ds(tok, tok), :], X.at[:, pl.ds(tok, tok), :], acts, actr, partner).wait_send()
    rcopy(rsc, rsc, scs, scr, far).wait_send()
    for hf in range(2):
        rcopy(rbuf.at[hf], rbuf.at[hf], rss.at[hf], rsr.at[hf], far).wait_send()
        for cp in zh_copies(hf):
            cp.wait_send()
        rcopy(res.at[hf, pl.ds(0, 7)], res.at[hf, pl.ds(0, 7)], ags.at[hf], agr.at[hf], far).wait_send()
    pcopy.wait_send()
    for cp in outs:
        cp.wait()


def body(
    activations, local_weights, grad_codes, block_scales, global_weights, momentum, block_owner
):
    tok, model = activations.shape
    rows, width = local_weights.shape[1:]
    nk = NX * NZ
    cut = (NY, 2, rows // (2 * NY), width)
    any_space = pl.BlockSpec(memory_space=pl.ANY)
    vmem = pl.BlockSpec(memory_space=pltpu.VMEM)
    bf, f32 = jnp.bfloat16, jnp.float32
    dma = pltpu.SemaphoreType.DMA
    proj, og, om = pl.pallas_call(
        gather_kernel,
        out_shape=(
            jax.ShapeDtypeStruct((tok, width), bf),
            jax.ShapeDtypeStruct(cut, bf),
            jax.ShapeDtypeStruct(cut, bf),
        ),
        in_specs=[any_space] * 7,
        out_specs=(vmem, any_space, any_space),
        scratch_shapes=[
            pltpu.VMEM((nk, 2 * tok, rows), bf),
            pltpu.VMEM((nk, rows, width), bf),
            pltpu.VMEM((2 * tok, width), f32),
            pltpu.VMEM((tok, width), f32),
            pltpu.VMEM(cut, jnp.int32),
            pltpu.VMEM((NY, 2, 32, width), bf),
            pltpu.VMEM((2, NY - 1, 32, width), bf),
            pltpu.VMEM((4, rows), f32),
            pltpu.VMEM((NY - 1, 4, 128), f32),
            pltpu.VMEM((4, rows), jnp.int32),
            pltpu.VMEM((2, 16, width), bf),
            pltpu.VMEM((128, 128), f32),
            pltpu.VMEM((128, 128), f32),
            pltpu.VMEM((2, 16, width), f32),
            pltpu.VMEM((2, 16, width), bf),
            pltpu.VMEM((2, 16, width), f32),
            pltpu.VMEM((2, 16, width), bf),
            pltpu.VMEM((2, NY, 2, 16, width), bf),
            dma((7,)),
            dma((NZ, 2, 2)), dma((NZ, 2, 2)),
            dma((NZ, 6)), dma((NZ, 6)),
            dma((4,)), dma((4,)),
            dma((NZ, 2)), dma((NZ, 2)),
            dma, dma,
            dma, dma,
            dma((2,)), dma((2,)),
            dma, dma,
            dma((2, 2)), dma((2, 2)),
            dma((2,)), dma((2,)),
            dma((2, 2)),
        ],
        compiler_params=pltpu.CompilerParams(
            collective_id=0, has_side_effects=True, vmem_limit_bytes=40 * 2**20
        ),
        name="sync_and_project",
    )(
        activations,
        local_weights[0],
        grad_codes[0].reshape(cut),
        block_scales[0].T,
        block_owner.T,
        global_weights.reshape(cut),
        momentum[0].reshape(cut),
    )
    return proj, og.reshape(rows, width), om.reshape(rows, width)


def solution(mesh):
    return jax.shard_map(
        body,
        mesh=mesh,
        in_specs=(
            P(("island", "fsdp"), None),
            P("island", "fsdp", None),
            P("island", "fsdp", None),
            P("island", "fsdp", None),
            P("fsdp", None),
            P("island", "fsdp", None),
            P("fsdp", None),
        ),
        out_specs=(P(("island", "fsdp"), None), P("fsdp", None), P("fsdp", None)),
        check_vma=False,
    )
```

time: 425 us -> 61.6 us (0.14)
  the two profiles are of different devices: /device:TPU:2 before, /device:TPU:6 now
where the time goes in v1:
time: 61.6 us; the launch traced here: 61.3 us
  Pallas kernels  51.4 us (83%)
  local copies, waits for them, and re-layouts  9.23 us (15%)
  between operations  0.66 us (1%)
    pallas_call x1, Pallas kernels, body(): pl.pallas_call(gather_kernel, out_shape=(jax.ShapeDtypeStruct((tok, width...  51.4 us
    unnamed x17, local copies, waits for them, and re-layouts  9.23 us

profile of v1, /device:TPU:6, one launch (start us, length us, event | category | flops | bytes accessed | tf_op | source)
XLA Modules:
  0.0 61.3 jit_solution(5426249080764880276)
XLA Ops:
  0.6 0.0 copy-start
  0.6 1.9 %copy-done = bf16[192,8192]{1,0:T(8,128)(2,1)S(1)} copy-done((bf16[192,8192]{1,0:T(8,128)(2,1)S(1)}, bf16[192,8192]{1,0:T(8,128)(2,1)}, u32[]{:S(2)}) %copy-start) | copy-done | bytes 3145752
  2.5 0.0 copy-start.1
  2.5 1.0 %copy-done.1 = s32[1,256,512]{2,1,0:T(8,128)S(1)} copy-done((s32[1,256,512]{2,1,0:T(8,128)S(1)}, s32[1,256,512]{2,1,0:T(8,128)}, u32[]{:S(2)}) %copy-start.1) | copy-done | bytes 524312
  3.6 0.0 copy-start.2
  3.6 0.9 %copy-done.2 = bf16[1,256,512]{2,1,0:T(8,128)(2,1)S(1)} copy-done((bf16[1,256,512]{2,1,0:T(8,128)(2,1)S(1)}, bf16[1,256,512]{2,1,0:T(8,128)(2,1)}, u32[]{:S(2)}) %copy-start.2) | copy-done | bytes 262168
  4.5 0.0 copy-start.3
  4.5 0.9 %copy-done.3 = bf16[256,512]{1,0:T(8,128)(2,1)S(1)} copy-done((bf16[256,512]{1,0:T(8,128)(2,1)S(1)}, bf16[256,512]{1,0:T(8,128)(2,1)}, u32[]{:S(2)}) %copy-start.3) | copy-done | bytes 262168
  5.5 0.0 copy-start.4
  5.5 0.9 %copy-done.4 = bf16[1,256,512]{2,1,0:T(8,128)(2,1)S(1)} copy-done((bf16[1,256,512]{2,1,0:T(8,128)(2,1)S(1)}, bf16[1,256,512]{2,1,0:T(8,128)(2,1)}, u32[]{:S(2)}) %copy-start.4) | copy-done | bytes 262168
  6.4 0.0 copy-start.5
  6.4 0.7 %copy-done.5 = f32[1,256,4]{1,2,0:T(4,128)S(1)} copy-done((f32[1,256,4]{1,2,0:T(4,128)S(1)}, f32[1,256,4]{1,2,0:T(4,128)}, u32[]{:S(2)}) %copy-start.5) | copy-done | bytes 4120
  7.1 0.0 copy-start.6
  7.1 0.7 %copy-done.6 = s32[256,4]{0,1:T(4,128)S(1)} copy-done((s32[256,4]{0,1:T(4,128)S(1)}, s32[256,4]{0,1:T(4,128)}, u32[]{:S(2)}) %copy-start.6) | copy-done | bytes 4120
  7.8 51.4 %sync_and_project.1 = (bf16[192,512]{1,0:T(8,128)(2,1)S(1)}, bf16[8,2,16,512]{3,2,1,0:T(8,128)(2,1)S(1)}, bf16[8,2,16,512]{3,2,1,0:T(8,128)(2,1)S(1)}) custom-call(bf16[192,8192]{1,0:T(8,128)(2,1)S(1)} %copy-done, bf16[256,512]{1,0:T(8,128)(2,1)S(1)} %bitcast.11, s32[8,2,16,512]{3,2,1,0:T(8,128)S(1)} %bitcast.10, f32[4,256]{1,0:T(4,128)S(1)} %bitcast.16, ...), custom_call_target="tpu_custom_call" | custom-call | tf_op jit(solution)/shard_map/sync_and_project/pallas_call | solution.py:386
  59.2 0.7 %copy.13 = bf16[192,512]{1,0:T(8,128)(2,1)} copy(bf16[192,512]{1,0:T(8,128)(2,1)S(1)} %get-tuple-element.12) | data formatting | bytes 393216
  59.9 0.7 %copy.14 = bf16[256,512]{1,0:T(8,128)(2,1)} copy(bf16[256,512]{1,0:T(8,128)(2,1)S(1)} %bitcast.15) | data formatting | bytes 524288
  60.6 0.7 %copy.15 = bf16[256,512]{1,0:T(8,128)(2,1)} copy(bf16[256,512]{1,0:T(8,128)(2,1)S(1)} %bitcast.14) | data formatting | bytes 524288
Async XLA Ops:
  0.6 1.9 %copy-start = (bf16[192,8192]{1,0:T(8,128)(2,1)S(1)}, bf16[192,8192]{1,0:T(8,128)(2,1)}, u32[]{:S(2)}) copy-start(bf16[192,8192]{1,0:T(8,128)(2,1)} %act.1) | copy-start | bytes 9437188
  2.5 1.0 %copy-start.1 = (s32[1,256,512]{2,1,0:T(8,128)S(1)}, s32[1,256,512]{2,1,0:T(8,128)}, u32[]{:S(2)}) copy-start(s32[1,256,512]{2,1,0:T(8,128)} %param.9) | copy-start | bytes 1572868
  3.6 0.9 %copy-start.2 = (bf16[1,256,512]{2,1,0:T(8,128)(2,1)S(1)}, bf16[1,256,512]{2,1,0:T(8,128)(2,1)}, u32[]{:S(2)}) copy-start(bf16[1,256,512]{2,1,0:T(8,128)(2,1)} %param.8) | copy-start | bytes 786436
  4.5 0.9 %copy-start.3 = (bf16[256,512]{1,0:T(8,128)(2,1)S(1)}, bf16[256,512]{1,0:T(8,128)(2,1)}, u32[]{:S(2)}) copy-start(bf16[256,512]{1,0:T(8,128)(2,1)} %param.11) | copy-start | bytes 786436
  5.5 0.9 %copy-start.4 = (bf16[1,256,512]{2,1,0:T(8,128)(2,1)S(1)}, bf16[1,256,512]{2,1,0:T(8,128)(2,1)}, u32[]{:S(2)}) copy-start(bf16[1,256,512]{2,1,0:T(8,128)(2,1)} %param.12) | copy-start | bytes 786436
  6.4 0.7 %copy-start.5 = (f32[1,256,4]{1,2,0:T(4,128)S(1)}, f32[1,256,4]{1,2,0:T(4,128)}, u32[]{:S(2)}) copy-start(f32[1,256,4]{1,2,0:T(4,128)} %param.10) | copy-start | bytes 12292
  7.1 0.7 %copy-start.6 = (s32[256,4]{0,1:T(4,128)S(1)}, s32[256,4]{0,1:T(4,128)}, u32[]{:S(2)}) copy-start(s32[256,4]{0,1:T(4,128)} %param.13) | copy-start | bytes 12292

commit v2 on v1

--- a/solution.py
+++ b/solution.py
@@ -22,7 +22,7 @@
     X, W, acc, pacc,
     cbuf, stg, rbuf, scbuf, rsc, owbuf, gbuf, tmp, tmpt, zs, zm, zrs, zrm, res,
     lsem, zsem_s, zsem_r, xsem_s, xsem_r, qxs, qxr, qzs, qzr,
-    acts, actr, pts, ptr_, rss, rsr, scs, scr, zhs, zhr, ags, agr, osem,
+    acts, actr, pts, ptr_, rss, rsr, scs, scr, zhs, zhr, ags, agr, osem, farsem, heresem,
 ):
     i, f = lax.axis_index("island"), lax.axis_index("fsdp")
     zh, y = i // NY, i % NY
@@ -49,11 +49,46 @@
             src_ref=src, dst_ref=dst, send_sem=ss, recv_sem=rs, device_id=dev, device_id_type=MESH
         )
 
+    g = y // 5
+    rank = (1 - g) * (2 * y - 1 + (NY - y) // NY) + g * 2 * (NY - y)
+
+    def rank_of(t):
+        gt = t // 5
+        return (1 - gt) * (2 * t - 1 + (NY - t) // NY) + gt * 2 * (NY - t)
+
+    up, down = fs(z + 1, x, c), fs(z - 1, x, c)
+    bar = pltpu.get_barrier_semaphore()
+
+    def hello(dev):
+        pl.semaphore_signal(bar, inc=1, device_id=dev, device_id_type=MESH)
+
+    ld_w = pltpu.make_async_copy(wown, W.at[z * NX + x], lsem.at[1])
+    ld_w.start()
+    for dev in (right, left, partner):
+        hello(dev)
+
+    @pl.when(z < NZ - 1)
+    def _():
+        hello(up)
+
+    @pl.when(z > 0)
+    def _():
+        hello(down)
+
+    for d in range(1, NY):
+        t = (y + d) % NY
+
+        @pl.when(rank_of(t) > rank)
+        def _():
+            hello(isl(zh, t))
+
+    @pl.when(zh == 0)
+    def _():
+        hello(far)
+
     kown = z * NX + x
     ld_codes = pltpu.make_async_copy(codes, cbuf, lsem.at[0])
     ld_codes.start()
-    ld_w = pltpu.make_async_copy(wown, W.at[kown], lsem.at[1])
-    ld_w.start()
     ld_mom = pltpu.make_async_copy(mom, stg.at[:, :, pl.ds(16, 16), :], lsem.at[2])
     ld_mom.start()
     ld_sc = pltpu.make_async_copy(scales, scbuf, lsem.at[3])
@@ -63,34 +98,44 @@
     ld_gw = pltpu.make_async_copy(gw.at[y], gbuf, lsem.at[5])
     ld_gw.start()
 
-    @pl.loop(0, NX * NZ)
-    def _(k):
-        col = pl.multiple_of((2 * k + c) * depth, depth)
-        pltpu.make_async_copy(
-            act.at[:, pl.ds(col, depth)], X.at[k, pl.ds(0, tok), :], lsem.at[6]
-        ).start()
-
-    bar = pltpu.get_barrier_semaphore()
-    zg = zh * NZ + z
-    zup, zdn = (zg + 1) % (2 * NZ), (zg + 2 * NZ - 1) % (2 * NZ)
-    peers = [right, left, partner, far]
-    peers += [isl(zh, (y + d) % NY) for d in range(1, NY)]
-    peers += [
-        {"island": (n // NZ) * NY + y, "fsdp": (n % NZ) * 2 * NX + x * 2 + c} for n in (zup, zdn)
-    ]
-    for dev in peers:
-        pl.semaphore_signal(bar, inc=1, device_id=dev, device_id_type=MESH)
-
-    ld_codes.wait()
-
-    @pl.loop(0, NY)
-    def _(t):
-        stg[t, :, pl.ds(0, 16), :] = cbuf[t].astype(jnp.float32).astype(jnp.bfloat16)
-
+    edge = 1 - (z + 1) // NZ + (z + NZ - 1) // NZ
     ld_w.wait()
-    ld_mom.wait()
-    ld_sc.wait()
-    pl.semaphore_wait(bar, len(peers))
+    pl.semaphore_wait(bar, 3 + edge + rank + zh)
+
+    def answer():
+        for d in range(1, NY):
+            t = (y + d) % NY
+
+            @pl.when(rank_of(t) < rank)
+            def _():
+                pl.semaphore_signal(heresem, inc=1, device_id=isl(zh, t), device_id_type=MESH)
+
+        @pl.when(zh == 1)
+        def _():
+            pl.semaphore_signal(farsem, inc=1, device_id=far, device_id_type=MESH)
+
+    def x_start():
+        @pl.loop(0, NX * NZ)
+        def _(k):
+            col = pl.multiple_of((2 * k + c) * depth, depth)
+            pltpu.make_async_copy(
+                act.at[:, pl.ds(col, depth)], X.at[k, pl.ds(0, tok), :], lsem.at[6]
+            ).start()
+
+    def codes_ready():
+        ld_codes.wait()
+
+        @pl.loop(0, NY)
+        def _(t):
+            stg[t, :, pl.ds(0, 16), :] = cbuf[t].astype(jnp.float32).astype(jnp.bfloat16)
+
+        ld_mom.wait()
+        ld_sc.wait()
+
+    def peers_here():
+        @pl.when(rank < NY - 1)
+        def _():
+            pl.semaphore_wait(heresem, NY - 1 - rank)
 
     def half(k, h):
         return W.at[k, pl.ds(h * hp, hp), :]
@@ -134,8 +179,6 @@
         k = z * NX + [xl, xr, xo, xo][n]
         ref = qpart(k) if n < 2 else qhalf(k, n - 2)
         return rcopy(ref, ref, qxs.at[n], qxr.at[n], right)
-
-    up, down = fs(z + 1, x, c), fs(z - 1, x, c)
 
     def zcopy(s, h, d):
         k = (z - s if d == 0 else z + s) * NX + x
@@ -274,46 +317,128 @@
         for d in far_first:
             ag_copy(hf, d).start()
 
-    qxcopy(0).start()
-    qxcopy(1).start()
-    xsend(0)
-    for h in range(2):
+    def zstart():
+        for h in range(2):
+            for d in range(2):
+                @pl.when(goes(d))
+                def _():
+                    zcopy(0, h, d).start()
+
+    def qzstart():
         for d in range(2):
             @pl.when(goes(d))
             def _():
-                zcopy(0, h, d).start()
-    for hf in range(2):
+                qzcopy(0, d).start()
+
+    def rs_start(hf):
         for d in far_first:
             rs_copy(hf, d).start()
-        if hf == 0:
-            for d in far_first:
-                sc_copy(d).start()
-
-    @pl.loop(0, NX * NZ)
-    def _(k):
-        col = pl.multiple_of((2 * k + 1 - c) * depth, depth)
-        rcopy(act.at[:, pl.ds(col, depth)], X.at[k, pl.ds(tok, tok), :], acts, actr, partner).start()
-
-    for n in range(2):
-        qxlanded(n).wait_recv()
-        qxcopy(2 + n).start()
+
+    def sc_start():
+        for d in far_first:
+            sc_copy(d).start()
+
+    def act_start():
+        @pl.loop(0, NX * NZ)
+        def _(k):
+            col = pl.multiple_of((2 * k + 1 - c) * depth, depth)
+            rcopy(act.at[:, pl.ds(col, depth)], X.at[k, pl.ds(tok, tok), :], acts, actr, partner).start()
+
+    act_in = rcopy(X.at[:, pl.ds(tok, tok), :], X.at[:, pl.ds(tok, tok), :], acts, actr, partner)
+
+    def act_wait():
+        act_in.wait_recv()
+        pltpu.make_async_copy(X.at[:, pl.ds(0, tok), :], X.at[:, pl.ds(0, tok), :], lsem.at[6]).wait()
+
+    def qstart():
+        qxcopy(0).start()
+        qxcopy(1).start()
+
+    def qpass():
+        for n in range(2):
+            qxlanded(n).wait_recv()
+            qxcopy(2 + n).start()
+
+    def qdone():
+        for n in (2, 3):
+            qxlanded(n).wait_recv()
+
+    def far_here():
+        @pl.when(zh == 0)
+        def _():
+            pl.semaphore_wait(farsem, 1)
+
+    pcopy = rcopy(acc.at[pl.ds(tok, tok), :], pacc, pts, ptr_, partner)
+    res_in = [
+        rcopy(res.at[hf, pl.ds(0, 7)], res.at[hf, pl.ds(0, 7)], ags.at[hf], agr.at[hf], far)
+        for hf in range(2)
+    ]
+    outs = [
+        pltpu.make_async_copy(res.at[hf, :, n], out.at[:, hf], osem.at[hf, n])
+        for hf in range(2)
+        for n, out in enumerate((og, om))
+    ]
+
+    def gathered(hf):
+        res_in[hf].wait_recv()
+        outs[2 * hf].start()
+        outs[2 * hf + 1].start()
+
+    def finish_proj():
+        pcopy.wait_recv()
+        proj[...] = (acc[pl.ds(0, tok), :] + pacc[...]).astype(jnp.bfloat16)
+
+    def sent_a():
+        for j in range(NZ):
+            for n in range(6):
+                xcopy(j, n).wait_send()
+        for n in range(4):
+            qxcopy(n).wait_send()
+        for s in range(NZ - 1):
+            for d in range(2):
+                @pl.when(has(s, d) & goes(d))
+                def _():
+                    for h in range(2):
+                        zcopy(s, h, d).wait_send()
+                    qzcopy(s, d).wait_send()
+        act_in.wait_send()
+        pcopy.wait_send()
+
+    def sent_b():
+        rcopy(rsc, rsc, scs, scr, far).wait_send()
+        for hf in range(2):
+            rcopy(rbuf.at[hf], rbuf.at[hf], rss.at[hf], rsr.at[hf], far).wait_send()
+            for cp in zh_copies(hf):
+                cp.wait_send()
+            res_in[hf].wait_send()
+        for cp in outs:
+            cp.wait()
+
+    qstart()
+    xsend(0)
+    zstart()
+    answer()
+    codes_ready()
+    peers_here()
+    rs_start(0)
+    sc_start()
+    rs_start(1)
+    act_start()
+    x_start()
+    qpass()
     zpass(1)
     xsend(1)
     xpass(0)
-    for n in (2, 3):
-        qxlanded(n).wait_recv()
-    for d in range(2):
-        @pl.when(goes(d))
-        def _():
-            qzcopy(0, d).start()
+    qdone()
+    qzstart()
     small_columns()
+    far_here()
     partial(0)
     zpass(2)
     xsend(2)
     xpass(1)
     xdone(0)
-    rcopy(X.at[:, pl.ds(tok, tok), :], X.at[:, pl.ds(tok, tok), :], acts, actr, partner).wait_recv()
-    pltpu.make_async_copy(X.at[:, pl.ds(0, tok), :], X.at[:, pl.ds(0, tok), :], lsem.at[6]).wait()
+    act_wait()
     acc[...] = jnp.zeros_like(acc)
     partial(1)
     zpass(3)
@@ -333,42 +458,20 @@
     multiply_row(2)
     xdone(3)
     multiply_row(3)
-
-    pcopy = rcopy(acc.at[pl.ds(tok, tok), :], pacc, pts, ptr_, partner)
     pcopy.start()
-    for hf in range(2):
-        rcopy(res.at[hf, pl.ds(0, 7)], res.at[hf, pl.ds(0, 7)], ags.at[hf], agr.at[hf], far).wait_recv()
-    outs = []
-    for hf in range(2):
-        for n, out in enumerate((og, om)):
-            cp = pltpu.make_async_copy(res.at[hf, :, n], out.at[:, hf], osem.at[hf, n])
-            cp.start()
-            outs.append(cp)
-    pcopy.wait_recv()
-    proj[...] = (acc[pl.ds(0, tok), :] + pacc[...]).astype(jnp.bfloat16)
-
-    for j in range(NZ):
-        for n in range(6):
-            xcopy(j, n).wait_send()
-    for n in range(4):
-        qxcopy(n).wait_send()
-    for s in range(NZ):
-        for d in range(2):
-            if s < NZ - 1:
-                @pl.when(has(s, d) & goes(d))
-                def _():
-                    for h in range(2):
-                        zcopy(s, h, d).wait_send()
-                    qzcopy(s, d).wait_send()
-    rcopy(X.at[:, pl.ds(tok, tok), :], X.at[:, pl.ds(tok, tok), :], acts, actr, partner).wait_send()
-    rcopy(rsc, rsc, scs, scr, far).wait_send()
-    for hf in range(2):
-        rcopy(rbuf.at[hf], rbuf.at[hf], rss.at[hf], rsr.at[hf], far).wait_send()
-        for cp in zh_copies(hf):
-            cp.wait_send()
-        rcopy(res.at[hf, pl.ds(0, 7)], res.at[hf, pl.ds(0, 7)], ags.at[hf], agr.at[hf], far).wait_send()
-    pcopy.wait_send()
-    for cp in outs:
+    gathered(0)
+    gathered(1)
+    finish_proj()
+    sent_a()
+    sent_b()
+
+
+def hand_over(*refs):
+    sem = refs[6]
+    copies = [pltpu.make_async_copy(refs[n], refs[n + 3], sem.at[n]) for n in range(3)]
+    for cp in copies:
+        cp.start()
+    for cp in copies:
         cp.wait()
 
 
@@ -381,17 +484,18 @@
     cut = (NY, 2, rows // (2 * NY), width)
     any_space = pl.BlockSpec(memory_space=pl.ANY)
     vmem = pl.BlockSpec(memory_space=pltpu.VMEM)
+    hbm = functools.partial(pltpu.with_memory_space_constraint, memory_space=pltpu.HBM)
     bf, f32 = jnp.bfloat16, jnp.float32
     dma = pltpu.SemaphoreType.DMA
     proj, og, om = pl.pallas_call(
         gather_kernel,
         out_shape=(
-            jax.ShapeDtypeStruct((tok, width), bf),
-            jax.ShapeDtypeStruct(cut, bf),
-            jax.ShapeDtypeStruct(cut, bf),
+            pltpu.VMEM((tok, width), bf),
+            pltpu.VMEM(cut, bf),
+            pltpu.VMEM(cut, bf),
         ),
         in_specs=[any_space] * 7,
-        out_specs=(vmem, any_space, any_space),
+        out_specs=(vmem, vmem, vmem),
         scratch_shapes=[
             pltpu.VMEM((nk, 2 * tok, rows), bf),
             pltpu.VMEM((nk, rows, width), bf),
@@ -423,21 +527,35 @@
             dma((2, 2)), dma((2, 2)),
             dma((2,)), dma((2,)),
             dma((2, 2)),
+            pltpu.SemaphoreType.REGULAR,
+            pltpu.SemaphoreType.REGULAR,
         ],
         compiler_params=pltpu.CompilerParams(
-            collective_id=0, has_side_effects=True, vmem_limit_bytes=40 * 2**20
+            collective_id=0, has_side_effects=True, vmem_limit_bytes=48 * 2**20
         ),
         name="sync_and_project",
     )(
-        activations,
-        local_weights[0],
-        grad_codes[0].reshape(cut),
-        block_scales[0].T,
-        block_owner.T,
-        global_weights.reshape(cut),
-        momentum[0].reshape(cut),
+        hbm(activations),
+        hbm(local_weights[0]),
+        hbm(grad_codes[0].reshape(cut)),
+        hbm(block_scales[0].T),
+        hbm(block_owner.T),
+        hbm(global_weights.reshape(cut)),
+        hbm(momentum[0].reshape(cut)),
     )
-    return proj, og.reshape(rows, width), om.reshape(rows, width)
+    return pl.pallas_call(
+        hand_over,
+        out_shape=(
+            jax.ShapeDtypeStruct((tok, width), bf),
+            jax.ShapeDtypeStruct((rows, width), bf),
+            jax.ShapeDtypeStruct((rows, width), bf),
+        ),
+        in_specs=[vmem] * 3,
+        out_specs=[any_space] * 3,
+        scratch_shapes=[dma((3,))],
+        compiler_params=pltpu.CompilerParams(vmem_limit_bytes=16 * 2**20),
+        name="hand_over",
+    )(proj, og.reshape(rows, width), om.reshape(rows, width))
 
 
 def solution(mesh):

time: 61.6 us -> 48.7 us (0.79)
  the two profiles are of different devices: /device:TPU:6 before, /device:TPU:1 now
where the time goes in v2:
time: 48.7 us; the launch traced here: 48.6 us
  Pallas kernels  47.9 us (98%)
  between operations  0.64 us (1%)
    pallas_call x1, Pallas kernels, body(): pl.pallas_call(gather_kernel, out_shape=(pltpu.VMEM((tok, width), bf), pl...  47 us

profile of v2, /device:TPU:1, one launch (start us, length us, event | category | flops | bytes accessed | tf_op | source)
XLA Modules:
  0.0 48.6 jit_solution(15219458288511751610)
XLA Ops:
  0.6 47.0 %sync_and_project.1 = (bf16[192,512]{1,0:T(8,128)(2,1)S(1)}, bf16[8,2,16,512]{3,2,1,0:T(8,128)(2,1)S(1)}, bf16[8,2,16,512]{3,2,1,0:T(8,128)(2,1)S(1)}) custom-call(bf16[192,8192]{1,0:T(8,128)(2,1)} %act.1, bf16[256,512]{1,0:T(8,128)(2,1)} %bitcast.13, s32[8,2,16,512]{3,2,1,0:T(8,128)} %bitcast.12, f32[4,256]{1,0:T(4,128)} %bitcast.16, s32[4,256]{1,0:T(4,128)} %bitcast.17, ...), custom_call_target="tpu_custom_call" | custom-call | tf_op jit(solution)/shard_map/sync_and_project/pallas_call | solution.py:490
  47.7 0.9 %hand_over.1 = (bf16[192,512]{1,0:T(8,128)(2,1)}, bf16[256,512]{1,0:T(8,128)(2,1)}, bf16[256,512]{1,0:T(8,128)(2,1)}) custom-call(bf16[192,512]{1,0:T(8,128)(2,1)S(1)} %get-tuple-element.6.refs_0_, bf16[256,512]{1,0:T(8,128)(2,1)S(1)} %bitcast.10, bf16[256,512]{1,0:T(8,128)(2,1)S(1)} %bitcast.11), custom_call_target="tpu_custom_call" | custom-call | tf_op jit(solution)/shard_map/hand_over/pallas_call | solution.py:546

commit v3 on v2

--- a/solution.py
+++ b/solution.py
@@ -13,23 +13,25 @@
 outer_rate = 0.7
 
 NX, NZ, NY = 4, 4, 8
-Q = 32
+NQ = 4
+Q = 16
+QF = 1 if Q < 32 else 2
 
 
 def gather_kernel(
     act, wown, codes, scales, owner, gw, mom,
-    proj, og, om,
+    proj, res,
     X, W, acc, pacc,
-    cbuf, stg, rbuf, scbuf, rsc, owbuf, gbuf, tmp, tmpt, zs, zm, zrs, zrm, res,
+    cbuf, stg, rbuf, scbuf, rsc, owbuf, gbuf, tmp, tmpt, zs, zm, zrs, zrm,
     lsem, zsem_s, zsem_r, xsem_s, xsem_r, qxs, qxr, qzs, qzr,
-    acts, actr, pts, ptr_, rss, rsr, scs, scr, zhs, zhr, ags, agr, osem, farsem, heresem,
+    acts, actr, pts, ptr_, rss, rsr, scs, scr, zhs, zhr, ags, agr, farsem, heresem,
 ):
     i, f = lax.axis_index("island"), lax.axis_index("fsdp")
     zh, y = i // NY, i % NY
     z, x, c = f // (2 * NX), (f // 2) % NX, f % 2
     rows = wown.shape[0]
     p = rows - Q
-    hp = p // 2
+    cut = p // 32 * 16
     tok = act.shape[0]
     depth = rows
 
@@ -89,8 +91,15 @@
     kown = z * NX + x
     ld_codes = pltpu.make_async_copy(codes, cbuf, lsem.at[0])
     ld_codes.start()
-    ld_mom = pltpu.make_async_copy(mom, stg.at[:, :, pl.ds(16, 16), :], lsem.at[2])
-    ld_mom.start()
+    hw = mom.shape[3] // 2
+    ld_mom = [
+        pltpu.make_async_copy(
+            mom.at[:, :, :, pl.ds(ch * hw, hw)], stg.at[:, :, ch, pl.ds(16, 16), :], lsem.at[(2, 7)[ch]]
+        )
+        for ch in range(2)
+    ]
+    for ld in ld_mom:
+        ld.start()
     ld_sc = pltpu.make_async_copy(scales, scbuf, lsem.at[3])
     ld_sc.start()
     ld_ow = pltpu.make_async_copy(owner, owbuf, lsem.at[4])
@@ -127,9 +136,12 @@
 
         @pl.loop(0, NY)
         def _(t):
-            stg[t, :, pl.ds(0, 16), :] = cbuf[t].astype(jnp.float32).astype(jnp.bfloat16)
-
-        ld_mom.wait()
+            for ch in range(2):
+                code = cbuf[t, :, :, pl.ds(ch * hw, hw)]
+                stg[t, :, ch, pl.ds(0, 16), :] = code.astype(jnp.float32).astype(jnp.bfloat16)
+
+        for ld in ld_mom:
+            ld.wait()
         ld_sc.wait()
 
     def peers_here():
@@ -137,14 +149,17 @@
         def _():
             pl.semaphore_wait(heresem, NY - 1 - rank)
 
-    def half(k, h):
-        return W.at[k, pl.ds(h * hp, hp), :]
+    def half(k, h, at=cut):
+        return W.at[k, pl.ds(h * at, at + h * (p - 2 * at)), :]
+
+    def xhalf(j, k, h):
+        return half(k, h, cut if j < NZ // 2 else p - cut)
 
     def qpart(k):
         return W.at[k, pl.ds(p, Q), :]
 
     def qhalf(k, h):
-        return W.at[k, pl.ds(p + h * (Q // 2), Q // 2), :]
+        return W.at[k, pl.ds(p + h * (Q // QF), Q // QF), :]
 
     def qrow(r):
         return W.at[pl.ds(r * NX, NX), pl.ds(p, Q), :]
@@ -162,12 +177,12 @@
             (r + x, 0, right), (r + x, 1, right), (r + x, 1, left), (r + x, 0, left),
             (r + xl, 0, right), (r + xr, 1, left),
         ][n]
-        return rcopy(half(k, h), half(k, h), xsem_s.at[j, n], xsem_r.at[j, n], dev)
+        return rcopy(xhalf(j, k, h), xhalf(j, k, h), xsem_s.at[j, n], xsem_r.at[j, n], dev)
 
     def xlanded(j, n):
         r = order(j) * NX
         k, h = [(r + xl, 0), (r + xl, 1), (r + xr, 1), (r + xr, 0), (r + xo, 0), (r + xo, 1)][n]
-        return rcopy(half(k, h), half(k, h), xsem_s.at[j, n], xsem_r.at[j, n], right)
+        return rcopy(xhalf(j, k, h), xhalf(j, k, h), xsem_s.at[j, n], xsem_r.at[j, n], right)
 
     def qxcopy(n):
         k = [kown, kown, z * NX + xl, z * NX + xr][n]
@@ -250,23 +265,42 @@
         def _(n):
             multiply(r + n)
 
-    def rs_copy(hf, d):
+    def last_row():
+        r = order(NZ - 1) * NX
+        multiply(r + x)
+        for n in (1, 3):
+            xlanded(NZ - 1, n).wait_recv()
+        multiply(r + xl)
+        multiply(r + xr)
+        for n in (4, 5):
+            xlanded(NZ - 1, n).wait_recv()
+        acc[pl.ds(tok, tok), :] += jnp.dot(
+            X[r + xo, pl.ds(tok, tok), :], W[r + xo], preferred_element_type=jnp.float32
+        )
+
+    def last_own():
+        r = order(NZ - 1) * NX
+        acc[pl.ds(0, tok), :] += jnp.dot(
+            X[r + xo, pl.ds(0, tok), :], W[r + xo], preferred_element_type=jnp.float32
+        )
+
+    def rs_copy(q, d):
         t = (y + d) % NY
-        return rcopy(stg.at[t, hf], rbuf.at[hf, d - 1], rss.at[hf], rsr.at[hf], isl(zh, t))
+        return rcopy(stg.at[t, q // 2, q % 2], rbuf.at[q, d - 1], rss.at[q], rsr.at[q], isl(zh, t))
 
     def sc_copy(d):
         t = (y + d) % NY
         lanes = pl.ds(pl.multiple_of((t // 4) * 128, 128), 128)
         return rcopy(scbuf.at[:, lanes], rsc.at[d - 1], scs, scr, isl(zh, t))
 
-    def zh_copies(hf):
+    def zh_copies(q):
         return (
-            rcopy(zs.at[hf], zrs.at[hf], zhs.at[hf, 0], zhr.at[hf, 0], far),
-            rcopy(zm.at[hf], zrm.at[hf], zhs.at[hf, 1], zhr.at[hf, 1], far),
+            rcopy(zs.at[q], zrs.at[q], zhs.at[q, 0], zhr.at[q, 0], far),
+            rcopy(zm.at[q], zrm.at[q], zhs.at[q, 1], zhr.at[q, 1], far),
         )
 
-    def ag_copy(hf, d):
-        return rcopy(res.at[hf, y], res.at[hf, y], ags.at[hf], agr.at[hf], isl(zh, (y + d) % NY))
+    def ag_copy(q, d):
+        return rcopy(res.at[q, y], res.at[q, y], ags.at[q], agr.at[q], isl(zh, (y + d) % NY))
 
     far_first = (4, 3, 5, 2, 6, 1, 7)
 
@@ -281,41 +315,46 @@
         tmp[pl.ds(32, 4), :] = owbuf[:, lanes].astype(jnp.float32)
         tmpt[...] = tmp[...].T
 
-    def partial(hf):
-        rcopy(rbuf.at[hf], rbuf.at[hf], rss.at[hf], rsr.at[hf], far).wait_recv()
-        cols = tmpt[pl.ds(pl.multiple_of(32 * (y % 4) + 16 * hf, 16), 16), :]
-        for b in range(4):
-            lanes = pl.ds(128 * b, 128)
+    def partial(q):
+        rcopy(rbuf.at[q], rbuf.at[q], rss.at[q], rsr.at[q], far).wait_recv()
+        cols = tmpt[pl.ds(pl.multiple_of(32 * (y % 4) + 16 * (q // 2), 16), 16), :]
+        for n in range(2):
+            lanes = pl.ds(128 * n, 128)
+            b = 2 * (q % 2) + n
             total = jnp.zeros((16, 128), jnp.float32)
             held = jnp.zeros((16, 128), jnp.float32)
             own = jnp.broadcast_to(cols[:, 32 + b : 33 + b], (16, 128))
             for d in range(NY):
                 if d == 0:
-                    code, state = stg[y, hf, pl.ds(0, 16), lanes], stg[y, hf, pl.ds(16, 16), lanes]
+                    code, state = (
+                        stg[y, q // 2, q % 2, pl.ds(0, 16), lanes],
+                        stg[y, q // 2, q % 2, pl.ds(16, 16), lanes],
+                    )
                 else:
                     code, state = (
-                        rbuf[hf, d - 1, pl.ds(0, 16), lanes],
-                        rbuf[hf, d - 1, pl.ds(16, 16), lanes],
+                        rbuf[q, d - 1, pl.ds(0, 16), lanes],
+                        rbuf[q, d - 1, pl.ds(16, 16), lanes],
                     )
                 total += code.astype(jnp.float32) * cols[:, 4 * d + b : 4 * d + b + 1]
                 who = (zh * NY + (y + NY - d) % NY).astype(jnp.float32)
                 held += jnp.where(own == who, state.astype(jnp.float32), 0.0)
-            zs[hf, :, lanes] = total
-            zm[hf, :, lanes] = held.astype(jnp.bfloat16)
-        for cp in zh_copies(hf):
+            zs[q, :, lanes] = total
+            zm[q, :, lanes] = held.astype(jnp.bfloat16)
+        for cp in zh_copies(q):
             cp.start()
 
-    def finish(hf):
-        for cp in zh_copies(hf):
+    def finish(q):
+        for cp in zh_copies(q):
             cp.wait_recv()
-        mean = (zs[hf] + zrs[hf]) * (1.0 / (2 * NY))
-        held = zm[hf].astype(jnp.float32) + zrm[hf].astype(jnp.float32)
+        mean = (zs[q] + zrs[q]) * (1.0 / (2 * NY))
+        held = zm[q].astype(jnp.float32) + zrm[q].astype(jnp.float32)
         fresh = outer_momentum * held + mean
-        updated = gbuf[hf].astype(jnp.float32) - outer_rate * (mean + outer_momentum * fresh)
-        res[hf, y, 0] = updated.astype(jnp.bfloat16)
-        res[hf, y, 1] = fresh.astype(jnp.bfloat16)
+        old = gbuf[q // 2, :, pl.ds((q % 2) * hw, hw)].astype(jnp.float32)
+        updated = old - outer_rate * (mean + outer_momentum * fresh)
+        res[q, y, 0] = updated.astype(jnp.bfloat16)
+        res[q, y, 1] = fresh.astype(jnp.bfloat16)
         for d in far_first:
-            ag_copy(hf, d).start()
+            ag_copy(q, d).start()
 
     def zstart():
         for h in range(2):
@@ -330,13 +369,12 @@
             def _():
                 qzcopy(0, d).start()
 
-    def rs_start(hf):
+    def rs_start(q):
+        if q == 0:
+            for d in far_first:
+                sc_copy(d).start()
         for d in far_first:
-            rs_copy(hf, d).start()
-
-    def sc_start():
-        for d in far_first:
-            sc_copy(d).start()
+            rs_copy(q, d).start()
 
     def act_start():
         @pl.loop(0, NX * NZ)
@@ -357,32 +395,24 @@
     def qpass():
         for n in range(2):
             qxlanded(n).wait_recv()
-            qxcopy(2 + n).start()
+            if n < QF:
+                qxcopy(2 + n).start()
 
     def qdone():
-        for n in (2, 3):
-            qxlanded(n).wait_recv()
+        for n in range(QF):
+            qxlanded(2 + n).wait_recv()
 
     def far_here():
-        @pl.when(zh == 0)
-        def _():
-            pl.semaphore_wait(farsem, 1)
+        pl.semaphore_wait(farsem, 1)
 
     pcopy = rcopy(acc.at[pl.ds(tok, tok), :], pacc, pts, ptr_, partner)
     res_in = [
-        rcopy(res.at[hf, pl.ds(0, 7)], res.at[hf, pl.ds(0, 7)], ags.at[hf], agr.at[hf], far)
-        for hf in range(2)
+        rcopy(res.at[q, pl.ds(0, 7)], res.at[q, pl.ds(0, 7)], ags.at[q], agr.at[q], far)
+        for q in range(NQ)
     ]
-    outs = [
-        pltpu.make_async_copy(res.at[hf, :, n], out.at[:, hf], osem.at[hf, n])
-        for hf in range(2)
-        for n, out in enumerate((og, om))
-    ]
-
-    def gathered(hf):
-        res_in[hf].wait_recv()
-        outs[2 * hf].start()
-        outs[2 * hf + 1].start()
+
+    def gathered(q):
+        res_in[q].wait_recv()
 
     def finish_proj():
         pcopy.wait_recv()
@@ -392,7 +422,7 @@
         for j in range(NZ):
             for n in range(6):
                 xcopy(j, n).wait_send()
-        for n in range(4):
+        for n in range(2 + QF):
             qxcopy(n).wait_send()
         for s in range(NZ - 1):
             for d in range(2):
@@ -406,69 +436,116 @@
 
     def sent_b():
         rcopy(rsc, rsc, scs, scr, far).wait_send()
-        for hf in range(2):
-            rcopy(rbuf.at[hf], rbuf.at[hf], rss.at[hf], rsr.at[hf], far).wait_send()
-            for cp in zh_copies(hf):
+        for q in range(NQ):
+            rcopy(rbuf.at[q], rbuf.at[q], rss.at[q], rsr.at[q], far).wait_send()
+            for cp in zh_copies(q):
                 cp.wait_send()
-            res_in[hf].wait_send()
-        for cp in outs:
-            cp.wait()
+            res_in[q].wait_send()
 
     qstart()
     xsend(0)
     zstart()
     answer()
     codes_ready()
-    peers_here()
-    rs_start(0)
-    sc_start()
-    rs_start(1)
     act_start()
     x_start()
+    @pl.when(zh == 1)
+    def _():
+        peers_here()
+
+    @pl.when(zh == 1)
+    def _():
+        rs_start(0)
+        rs_start(1)
+        rs_start(2)
+        rs_start(3)
+
     qpass()
     zpass(1)
     xsend(1)
+    @pl.when(zh == 0)
+    def _():
+        peers_here()
+
+    @pl.when(zh == 0)
+    def _():
+        rs_start(0)
+        rs_start(1)
+        rs_start(2)
+        rs_start(3)
+
     xpass(0)
     qdone()
     qzstart()
-    small_columns()
-    far_here()
-    partial(0)
+    @pl.when(zh == 1)
+    def _():
+        small_columns()
+        partial(0)
+        partial(1)
+
     zpass(2)
     xsend(2)
+    @pl.when(zh == 1)
+    def _():
+        partial(2)
+
     xpass(1)
+    qzpass(1)
+    @pl.when(zh == 1)
+    def _():
+        partial(3)
+
+    @pl.when(zh == 0)
+    def _():
+        far_here()
+
+    @pl.when(zh == 0)
+    def _():
+        small_columns()
+        partial(0)
+        partial(1)
+        partial(2)
+
     xdone(0)
     act_wait()
     acc[...] = jnp.zeros_like(acc)
-    partial(1)
+    multiply_row(0)
+    ld_gw.wait()
+    finish(0)
+    @pl.when(zh == 0)
+    def _():
+        partial(3)
+
     zpass(3)
     xsend(3)
-    multiply_row(0)
-    qzpass(1)
     xpass(2)
-    ld_gw.wait()
-    finish(0)
     qzpass(2)
+    finish(1)
+    qzpass(3)
     xdone(1)
-    qzpass(3)
     multiply_row(1)
+    finish(2)
     xpass(3)
-    finish(1)
+    finish(3)
     xdone(2)
     multiply_row(2)
-    xdone(3)
-    multiply_row(3)
+    last_row()
     pcopy.start()
-    gathered(0)
-    gathered(1)
+    last_own()
+    for q in range(NQ):
+        gathered(q)
     finish_proj()
     sent_a()
     sent_b()
 
 
-def hand_over(*refs):
-    sem = refs[6]
-    copies = [pltpu.make_async_copy(refs[n], refs[n + 3], sem.at[n]) for n in range(3)]
+def hand_over(proj, res, out, og, om, sem):
+    hw = res.shape[4]
+    copies = [pltpu.make_async_copy(proj, out, sem.at[0])]
+    for n, held in enumerate((og, om)):
+        for q in range(NQ):
+            part = held.at[:, q // 2, :, pl.ds(q % 2 * hw, hw)]
+            copies.append(pltpu.make_async_copy(res.at[q, :, n], part, sem.at[1 + NQ * n + q]))
     for cp in copies:
         cp.start()
     for cp in copies:
@@ -487,46 +564,43 @@
     hbm = functools.partial(pltpu.with_memory_space_constraint, memory_space=pltpu.HBM)
     bf, f32 = jnp.bfloat16, jnp.float32
     dma = pltpu.SemaphoreType.DMA
-    proj, og, om = pl.pallas_call(
+    proj, res = pl.pallas_call(
         gather_kernel,
         out_shape=(
             pltpu.VMEM((tok, width), bf),
-            pltpu.VMEM(cut, bf),
-            pltpu.VMEM(cut, bf),
+            pltpu.VMEM((NQ, NY, 2, 16, width // 2), bf),
         ),
         in_specs=[any_space] * 7,
-        out_specs=(vmem, vmem, vmem),
+        out_specs=(vmem, vmem),
         scratch_shapes=[
             pltpu.VMEM((nk, 2 * tok, rows), bf),
             pltpu.VMEM((nk, rows, width), bf),
             pltpu.VMEM((2 * tok, width), f32),
             pltpu.VMEM((tok, width), f32),
             pltpu.VMEM(cut, jnp.int32),
-            pltpu.VMEM((NY, 2, 32, width), bf),
-            pltpu.VMEM((2, NY - 1, 32, width), bf),
+            pltpu.VMEM((NY, 2, 2, 32, width // 2), bf),
+            pltpu.VMEM((NQ, NY - 1, 32, width // 2), bf),
             pltpu.VMEM((4, rows), f32),
             pltpu.VMEM((NY - 1, 4, 128), f32),
             pltpu.VMEM((4, rows), jnp.int32),
             pltpu.VMEM((2, 16, width), bf),
             pltpu.VMEM((128, 128), f32),
             pltpu.VMEM((128, 128), f32),
-            pltpu.VMEM((2, 16, width), f32),
-            pltpu.VMEM((2, 16, width), bf),
-            pltpu.VMEM((2, 16, width), f32),
-            pltpu.VMEM((2, 16, width), bf),
-            pltpu.VMEM((2, NY, 2, 16, width), bf),
-            dma((7,)),
+            pltpu.VMEM((NQ, 16, width // 2), f32),
+            pltpu.VMEM((NQ, 16, width // 2), bf),
+            pltpu.VMEM((NQ, 16, width // 2), f32),
+            pltpu.VMEM((NQ, 16, width // 2), bf),
+            dma((8,)),
             dma((NZ, 2, 2)), dma((NZ, 2, 2)),
             dma((NZ, 6)), dma((NZ, 6)),
             dma((4,)), dma((4,)),
             dma((NZ, 2)), dma((NZ, 2)),
             dma, dma,
             dma, dma,
-            dma((2,)), dma((2,)),
+            dma((NQ,)), dma((NQ,)),
             dma, dma,
-            dma((2, 2)), dma((2, 2)),
-            dma((2,)), dma((2,)),
-            dma((2, 2)),
+            dma((NQ, 2)), dma((NQ, 2)),
+            dma((NQ,)), dma((NQ,)),
             pltpu.SemaphoreType.REGULAR,
             pltpu.SemaphoreType.REGULAR,
         ],
@@ -543,19 +617,20 @@
         hbm(global_weights.reshape(cut)),
         hbm(momentum[0].reshape(cut)),
     )
-    return pl.pallas_call(
+    proj, og, om = pl.pallas_call(
         hand_over,
         out_shape=(
             jax.ShapeDtypeStruct((tok, width), bf),
-            jax.ShapeDtypeStruct((rows, width), bf),
-            jax.ShapeDtypeStruct((rows, width), bf),
+            jax.ShapeDtypeStruct(cut, bf),
+            jax.ShapeDtypeStruct(cut, bf),
         ),
-        in_specs=[vmem] * 3,
+        in_specs=[vmem] * 2,
         out_specs=[any_space] * 3,
-        scratch_shapes=[dma((3,))],
+        scratch_shapes=[dma((1 + 2 * NQ,))],
         compiler_params=pltpu.CompilerParams(vmem_limit_bytes=16 * 2**20),
         name="hand_over",
-    )(proj, og.reshape(rows, width), om.reshape(rows, width))
+    )(proj, res)
+    return proj, og.reshape(rows, width), om.reshape(rows, width)
 
 
 def solution(mesh):

time: 48.7 us -> 46.7 us (0.959)
  the two profiles are of different devices: /device:TPU:1 before, /device:TPU:64 now
where the time goes in v3:
time: 46.7 us; the launch traced here: 46.6 us
  Pallas kernels  45.9 us (98%)
  between operations  0.64 us (1%)
    pallas_call x1, Pallas kernels, body(): pl.pallas_call(gather_kernel, out_shape=(pltpu.VMEM((tok, width), bf), pl...  45 us

profile of v3, /device:TPU:64, one launch (start us, length us, event | category | flops | bytes accessed | tf_op | source)
XLA Modules:
  0.0 46.6 jit_solution(13531560156235772824)
XLA Ops:
  0.6 45.0 %sync_and_project.1 = (bf16[192,512]{1,0:T(8,128)(2,1)S(1)}, bf16[4,8,2,16,256]{4,3,2,1,0:T(8,128)(2,1)S(1)}) custom-call(bf16[192,8192]{1,0:T(8,128)(2,1)} %act.1, bf16[256,512]{1,0:T(8,128)(2,1)} %bitcast.11, s32[8,2,16,512]{3,2,1,0:T(8,128)} %bitcast.10, f32[4,256]{1,0:T(4,128)} %bitcast.14, s32[4,256]{1,0:T(4,128)} %bitcast.15, ...), custom_call_target="tpu_custom_call" | custom-call | tf_op jit(solution)/shard_map/sync_and_project/pallas_call | solution.py:567
  45.7 0.9 %hand_over.1 = (bf16[192,512]{1,0:T(8,128)(2,1)}, bf16[8,2,16,512]{3,2,1,0:T(8,128)(2,1)}, bf16[8,2,16,512]{3,2,1,0:T(8,128)(2,1)}) custom-call(bf16[192,512]{1,0:T(8,128)(2,1)S(1)} %get-tuple-element.8.proj, bf16[4,8,2,16,256]{4,3,2,1,0:T(8,128)(2,1)S(1)} %get-tuple-element.9.res), custom_call_target="tpu_custom_call" | custom-call | tf_op jit(solution)/shard_map/hand_over/pallas_call | solution.py:620

commit v4 on v3

--- a/solution.py
+++ b/solution.py
@@ -14,7 +14,7 @@
 
 NX, NZ, NY = 4, 4, 8
 NQ = 4
-Q = 16
+Q = 32
 QF = 1 if Q < 32 else 2
 
 
@@ -24,7 +24,7 @@
     X, W, acc, pacc,
     cbuf, stg, rbuf, scbuf, rsc, owbuf, gbuf, tmp, tmpt, zs, zm, zrs, zrm,
     lsem, zsem_s, zsem_r, xsem_s, xsem_r, qxs, qxr, qzs, qzr,
-    acts, actr, pts, ptr_, rss, rsr, scs, scr, zhs, zhr, ags, agr, farsem, heresem,
+    acts, actr, pts, ptr_, rss, rsr, scs, scr, zhs, zhr, ags, agr, farsem, heresem, upsem,
 ):
     i, f = lax.axis_index("island"), lax.axis_index("fsdp")
     zh, y = i // NY, i % NY
@@ -72,10 +72,6 @@
     @pl.when(z < NZ - 1)
     def _():
         hello(up)
-
-    @pl.when(z > 0)
-    def _():
-        hello(down)
 
     for d in range(1, NY):
         t = (y + d) % NY
@@ -107,9 +103,14 @@
     ld_gw = pltpu.make_async_copy(gw.at[y], gbuf, lsem.at[5])
     ld_gw.start()
 
-    edge = 1 - (z + 1) // NZ + (z + NZ - 1) // NZ
+    below = (z + NZ - 1) // NZ
     ld_w.wait()
-    pl.semaphore_wait(bar, 3 + edge + rank + zh)
+    pl.semaphore_wait(bar, 3 + below + rank + zh)
+
+    def zanswer():
+        @pl.when(z > 0)
+        def _():
+            pl.semaphore_signal(upsem, inc=1, device_id=down, device_id_type=MESH)
 
     def answer():
         for d in range(1, NY):
@@ -356,12 +357,13 @@
         for d in far_first:
             ag_copy(q, d).start()
 
-    def zstart():
-        for h in range(2):
-            for d in range(2):
-                @pl.when(goes(d))
-                def _():
-                    zcopy(0, h, d).start()
+    def zstart(d):
+        @pl.when(goes(d))
+        def _():
+            if d == 0:
+                pl.semaphore_wait(upsem, 1)
+            for h in range(2):
+                zcopy(0, h, d).start()
 
     def qzstart():
         for d in range(2):
@@ -415,7 +417,7 @@
         res_in[q].wait_recv()
 
     def finish_proj():
-        pcopy.wait_recv()
+        pcopy.wait()
         proj[...] = (acc[pl.ds(0, tok), :] + pacc[...]).astype(jnp.bfloat16)
 
     def sent_a():
@@ -432,7 +434,6 @@
                         zcopy(s, h, d).wait_send()
                     qzcopy(s, d).wait_send()
         act_in.wait_send()
-        pcopy.wait_send()
 
     def sent_b():
         rcopy(rsc, rsc, scs, scr, far).wait_send()
@@ -444,11 +445,13 @@
 
     qstart()
     xsend(0)
-    zstart()
+    zanswer()
+    zstart(1)
     answer()
     codes_ready()
     act_start()
     x_start()
+    zstart(0)
     @pl.when(zh == 1)
     def _():
         peers_here()
@@ -461,8 +464,6 @@
         rs_start(3)
 
     qpass()
-    zpass(1)
-    xsend(1)
     @pl.when(zh == 0)
     def _():
         peers_here()
@@ -474,6 +475,8 @@
         rs_start(2)
         rs_start(3)
 
+    zpass(1)
+    xsend(1)
     xpass(0)
     qdone()
     qzstart()
@@ -482,19 +485,16 @@
         small_columns()
         partial(0)
         partial(1)
+        partial(2)
 
     zpass(2)
     xsend(2)
     @pl.when(zh == 1)
     def _():
-        partial(2)
+        partial(3)
 
     xpass(1)
     qzpass(1)
-    @pl.when(zh == 1)
-    def _():
-        partial(3)
-
     @pl.when(zh == 0)
     def _():
         far_here()
@@ -521,7 +521,6 @@
     xpass(2)
     qzpass(2)
     finish(1)
-    qzpass(3)
     xdone(1)
     multiply_row(1)
     finish(2)
@@ -529,14 +528,15 @@
     finish(3)
     xdone(2)
     multiply_row(2)
+    qzpass(3)
     last_row()
     pcopy.start()
     last_own()
     for q in range(NQ):
         gathered(q)
-    finish_proj()
     sent_a()
     sent_b()
+    finish_proj()
 
 
 def hand_over(proj, res, out, og, om, sem):
@@ -603,6 +603,7 @@
             dma((NQ,)), dma((NQ,)),
             pltpu.SemaphoreType.REGULAR,
             pltpu.SemaphoreType.REGULAR,
+            pltpu.SemaphoreType.REGULAR,
         ],
         compiler_params=pltpu.CompilerParams(
             collective_id=0, has_side_effects=True, vmem_limit_bytes=48 * 2**20

time: 46.7 us -> 46.6 us (level)
  no operation moved by 1% of the time
where the time goes in v4:
time: 46.6 us; the launch traced here: 46.4 us
  Pallas kernels  45.8 us (98%)
  between operations  0.64 us (1%)
    pallas_call x1, Pallas kernels, body(): pl.pallas_call(gather_kernel, out_shape=(pltpu.VMEM((tok, width), bf), pl...  44.9 us

profile of v4, /device:TPU:64, one launch (start us, length us, event | category | flops | bytes accessed | tf_op | source)
XLA Modules:
  0.0 46.4 jit_solution(11131090696908361332)
XLA Ops:
  0.6 44.9 %sync_and_project.1 = (bf16[192,512]{1,0:T(8,128)(2,1)S(1)}, bf16[4,8,2,16,256]{4,3,2,1,0:T(8,128)(2,1)S(1)}) custom-call(bf16[192,8192]{1,0:T(8,128)(2,1)} %act.1, bf16[256,512]{1,0:T(8,128)(2,1)} %bitcast.11, s32[8,2,16,512]{3,2,1,0:T(8,128)} %bitcast.10, f32[4,256]{1,0:T(4,128)} %bitcast.14, s32[4,256]{1,0:T(4,128)} %bitcast.15, ...), custom_call_target="tpu_custom_call" | custom-call | tf_op jit(solution)/shard_map/sync_and_project/pallas_call | solution.py:567
  45.5 0.9 %hand_over.1 = (bf16[192,512]{1,0:T(8,128)(2,1)}, bf16[8,2,16,512]{3,2,1,0:T(8,128)(2,1)}, bf16[8,2,16,512]{3,2,1,0:T(8,128)(2,1)}) custom-call(bf16[192,512]{1,0:T(8,128)(2,1)S(1)} %get-tuple-element.8.proj, bf16[4,8,2,16,256]{4,3,2,1,0:T(8,128)(2,1)S(1)} %get-tuple-element.9.res), custom_call_target="tpu_custom_call" | custom-call | tf_op jit(solution)/shard_map/hand_over/pallas_call | solution.py:621

commit v5 on v4

--- a/solution.py
+++ b/solution.py
@@ -275,9 +275,12 @@
         multiply(r + xr)
         for n in (4, 5):
             xlanded(NZ - 1, n).wait_recv()
-        acc[pl.ds(tok, tok), :] += jnp.dot(
-            X[r + xo, pl.ds(tok, tok), :], W[r + xo], preferred_element_type=jnp.float32
-        )
+        for h in range(2):
+            cols = pl.ds(h * hw, hw)
+            acc[pl.ds(tok, tok), cols] += jnp.dot(
+                X[r + xo, pl.ds(tok, tok), :], W[r + xo, :, cols], preferred_element_type=jnp.float32
+            )
+            pcopy(h).start()
 
     def last_own():
         r = order(NZ - 1) * NX
@@ -407,7 +410,10 @@
     def far_here():
         pl.semaphore_wait(farsem, 1)
 
-    pcopy = rcopy(acc.at[pl.ds(tok, tok), :], pacc, pts, ptr_, partner)
+    def pcopy(h):
+        cols = pl.ds(h * hw, hw)
+        return rcopy(acc.at[pl.ds(tok, tok), cols], pacc.at[:, cols], pts.at[h], ptr_.at[h], partner)
+
     res_in = [
         rcopy(res.at[q, pl.ds(0, 7)], res.at[q, pl.ds(0, 7)], ags.at[q], agr.at[q], far)
         for q in range(NQ)
@@ -417,8 +423,10 @@
         res_in[q].wait_recv()
 
     def finish_proj():
-        pcopy.wait()
-        proj[...] = (acc[pl.ds(0, tok), :] + pacc[...]).astype(jnp.bfloat16)
+        for h in range(2):
+            cols = pl.ds(h * hw, hw)
+            pcopy(h).wait()
+            proj[:, cols] = (acc[pl.ds(0, tok), cols] + pacc[:, cols]).astype(jnp.bfloat16)
 
     def sent_a():
         for j in range(NZ):
@@ -530,7 +538,6 @@
     multiply_row(2)
     qzpass(3)
     last_row()
-    pcopy.start()
     last_own()
     for q in range(NQ):
         gathered(q)
@@ -596,7 +603,7 @@
             dma((4,)), dma((4,)),
             dma((NZ, 2)), dma((NZ, 2)),
             dma, dma,
-            dma, dma,
+            dma((2,)), dma((2,)),
             dma((NQ,)), dma((NQ,)),
             dma, dma,
             dma((NQ, 2)), dma((NQ, 2)),

time: 46.6 us -> 46.6 us (level)
  no operation moved by 1% of the time
where the time goes in v5:
time: 46.6 us; the launch traced here: 46.5 us
  Pallas kernels  45.8 us (98%)
  between operations  0.64 us (1%)
    pallas_call x1, Pallas kernels, body(): pl.pallas_call(gather_kernel, out_shape=(pltpu.VMEM((tok, width), bf), pl...  44.9 us

profile of v5, /device:TPU:64, one launch (start us, length us, event | category | flops | bytes accessed | tf_op | source)
XLA Modules:
  0.0 46.5 jit_solution(15724558624379491868)
XLA Ops:
  0.6 44.9 %sync_and_project.1 = (bf16[192,512]{1,0:T(8,128)(2,1)S(1)}, bf16[4,8,2,16,256]{4,3,2,1,0:T(8,128)(2,1)S(1)}) custom-call(bf16[192,8192]{1,0:T(8,128)(2,1)} %act.1, bf16[256,512]{1,0:T(8,128)(2,1)} %bitcast.11, s32[8,2,16,512]{3,2,1,0:T(8,128)} %bitcast.10, f32[4,256]{1,0:T(4,128)} %bitcast.14, s32[4,256]{1,0:T(4,128)} %bitcast.15, ...), custom_call_target="tpu_custom_call" | custom-call | tf_op jit(solution)/shard_map/sync_and_project/pallas_call | solution.py:574
  45.5 0.9 %hand_over.1 = (bf16[192,512]{1,0:T(8,128)(2,1)}, bf16[8,2,16,512]{3,2,1,0:T(8,128)(2,1)}, bf16[8,2,16,512]{3,2,1,0:T(8,128)(2,1)}) custom-call(bf16[192,512]{1,0:T(8,128)(2,1)S(1)} %get-tuple-element.8.proj, bf16[4,8,2,16,256]{4,3,2,1,0:T(8,128)(2,1)S(1)} %get-tuple-element.9.res), custom_call_target="tpu_custom_call" | custom-call | tf_op jit(solution)/shard_map/hand_over/pallas_call | solution.py:628
